TPU v7x, 256 devices: a whole 4x4x8 slice. The times are simulated.
256 devices in a mesh: rep: 4 (over z_hi, core), fsdp: 64 (over y, x, z_lo).
Axes of the slice: x: 4, y: 4, z: 8 (z_hi: 2, z_lo: 4; z = z_hi * 4 + z_lo), core: 2. Of those that a mesh axis runs over, the one named last changes fastest.
Arguments:
- features: bfloat16 [14336, 4096], P(('rep', 'fsdp')), may hold values from -6 to 6
- cotangent: bfloat16 [14336, 14336], P('rep', 'fsdp'), may hold values from -6 to 6
- up_rows: bfloat16 [14336, 4096], P('fsdp'), may hold values from -0.09375 to 0.09375
- moment: float32 [14336, 4096], P('fsdp'), may hold values from -4 to 4
- exponents: int32 [14336, 32], P('fsdp'), may hold values from -11 to -8
Outputs:
- new_params: bfloat16 [14336, 4096], P('fsdp')
- new_moment: float32 [14336, 4096], P('fsdp')
All inputs are finite; a program needn't handle non-finite values.
Results may differ from a plain program's by a relative error of at most 0.013.
Values may be sent and summed in bfloat16 or wider, within the bound.
A program may use at most 128 MiB of HBM per device.

v0:
```python
import jax
import jax.numpy as jnp
from jax import lax
from jax.sharding import PartitionSpec as P

inner_rate = 0.02
outer_rate = 0.7
momentum_coef = 0.9
code_limit = 448.0


def silu_slope(preact):
    squashed = jax.nn.sigmoid(preact)
    return squashed * (1.0 + preact * (1.0 - squashed))


def encode_blocks(gradient, scales):
    shard_rows, model_width = gradient.shape
    blocked = gradient.reshape(shard_rows, model_width // 128, 128) * jnp.exp2(-scales)[:, :, None]
    clipped = jnp.clip(inner_rate * blocked, -code_limit, code_limit).astype(jnp.bfloat16)
    return lax.optimization_barrier(clipped).astype(jnp.float32).reshape(shard_rows, model_width)


def nesterov_step(summed, scales, params, moment, groups):
    shard_rows, model_width = summed.shape
    blocked = summed.reshape(shard_rows, model_width // 128, 128) * jnp.exp2(scales)[:, :, None]
    decoded = blocked.reshape(shard_rows, model_width) / groups
    new_moment = momentum_coef * moment + decoded
    new_params = (
        params.astype(jnp.float32) - outer_rate * (decoded + momentum_coef * new_moment)
    ).astype(jnp.bfloat16)
    return (new_params, new_moment)


def per_device(features, cotangent, up_rows, moment, exponents):
    scales = exponents.astype(jnp.float32)
    inputs = lax.all_gather(features, "fsdp", axis=0, tiled=True)
    preact = jnp.einsum("td,fd->tf", inputs, up_rows, preferred_element_type=jnp.float32)
    hidden_grad = (cotangent.astype(jnp.float32) * silu_slope(preact)).astype(jnp.bfloat16)
    gradient = jnp.einsum("tf,td->fd", hidden_grad, inputs, preferred_element_type=jnp.float32)
    encoded = encode_blocks(gradient, scales)
    groups = lax.axis_size("rep")
    summed = lax.psum(encoded.astype(jnp.bfloat16), "rep").astype(jnp.float32)
    new_params, new_moment = nesterov_step(summed, scales, up_rows, moment, float(groups))
    return (new_params, new_moment)


def solution(mesh):
    return jax.shard_map(
        per_device,
        mesh=mesh,
        in_specs=(
            P(("rep", "fsdp"), None),
            P("rep", "fsdp"),
            P("fsdp", None),
            P("fsdp", None),
            P("fsdp", None),
        ),
        out_specs=(P("fsdp", None), P("fsdp", None)),
        check_vma=False,
    )
```

profile of v0, /device:TPU:1, one launch (start us, length us, event | category | flops | bytes accessed | tf_op | source)
XLA Modules:
  0.0 803.5 jit_solution(7693369832160337750)
XLA Ops:
  7.2 0.0 all-gather.2.cloned.1.call-start
  7.2 0.7 all-gather.2.cloned.1.call-update
  7.9 0.0 all-reduce.2.cloned.1.call-start
  7.9 0.8 multiply_exponential_fusion.1
  8.7 0.1 copy.7
  8.8 645.3 %all-gather.2.cloned.1.call-done = bf16[3584,4096]{1,0:T(8,128)(2,1)} async-done(((bf16[56,4096]{1,0:T(8,128)(2,1)}), bf16[3584,4096]{1,0:T(8,128)(2,1)}) %all-gather.2.cloned.1.call-update) | async-done | bytes 29360144 | tf_op jit(solution)/shard_map/all_gather | solution.py:37
  654.1 35.4 %convolution_bitcast_fusion = f32[28,8,32,128]{3,1,2,0:T(8,128)} fusion(bf16[3584,4096]{1,0:T(8,128)(2,1)} %all-gather.2.cloned.1.call-done, bf16[3584,224]{0,1:T(8,128)(2,1)} %param.6, bf16[224,4096]{1,0:T(8,128)(2,1)} %param.7), kind=kOutput, calls=%fused_computation.9 | convolution fusion | flops 13161365504 | bytes 36470784 | tf_op jit(solution)/shard_map/tf,td->fd/dot_general | solution.py:40
  689.5 2.7 copy.9
  692.2 1.4 fusion.3
  693.5 2.1 copy.19
  695.6 0.0 copy-start.1
  695.6 0.0 all-reduce.2.cloned.1.call-update
  695.6 0.1 copy.8
  695.7 90.9 %all-reduce.2.cloned.1.call-done = bf16[224,4096]{1,0:T(8,128)(2,1)} async-done(((bf16[224,4096]{1,0:T(8,128)(2,1)}), bf16[224,4096]{1,0:T(8,128)(2,1)}) %all-reduce.2.cloned.1.call-update) | async-done | bytes 1835024 | tf_op jit(solution)/shard_map/psum | solution.py:43
  786.6 0.0 copy-start
  786.6 1.0 mul.53
  787.6 0.0 copy-done.1
  787.6 1.0 copy-done
  788.6 8.0 subtract_convert_fusion
Async XLA Ops:
  7.2 647.0 %all-gather.2.cloned.1.call-start = ((), (), s32[]{:S(2)}) async-start(), calls=%async_computation | async-start | bytes 29818880 | tf_op jit(solution)/shard_map/all_gather | solution.py:37
  7.9 778.7 %all-reduce.2.cloned.1.call-start = ((), (), s32[]{:S(2)}) async-start(), calls=%async_computation.1 | async-start | bytes 3670016 | tf_op jit(solution)/shard_map/psum | solution.py:43
  695.6 92.0 %copy-start.1 = (bf16[224,4096]{1,0:T(8,128)(2,1)S(1)}, bf16[224,4096]{1,0:T(8,128)(2,1)}, u32[]{:S(2)}) copy-start(bf16[224,4096]{1,0:T(8,128)(2,1)} %param.7) | copy-start | bytes 5505028
  786.6 2.0 copy-start
Sparse Core Ops, SparseCore 0:
  9.8 644.2 all-gather.1
  695.8 90.8 all-reduce.1
where the time goes:
time: 804 us; the launch traced here: 803 us
  waiting for transfers between devices  737 us (92%)
  matrix products  35.4 us (4%)
  between operations  14.1 us (2%)
  other arithmetic  10.1 us (1%)
    all_gather x1, waiting for transfers between devices, per_device(): inputs = lax.all_gather(features, 'fsdp', axis=0, tiled=True)  645 us
    psum x1, waiting for transfers between devices, per_device(): summed = lax.psum(encoded.astype(jnp.bfloat16), 'rep').astype(jnp.float32)  90.9 us
    dot_general x1, matrix products, per_device(): jnp.einsum('tf,td->fd', hidden_grad, inputs, preferred_element_type=jnp.f...  35.4 us
  transfers between devices with their start and end apart: 2, of which 2 were waited for; matrix products, arithmetic and copies ran while one was open for 0% of the time, Pallas kernels for 0%

commit v1 on v0

v1 whole, which is shorter than its diff:
```python
import functools

import jax
import jax.numpy as jnp
from jax import lax
from jax.experimental import pallas as pl
from jax.experimental.pallas import tpu as pltpu
from jax.sharding import PartitionSpec as P

inner_rate = 0.02
outer_rate = 0.7
momentum_coef = 0.9
code_limit = 448.0

D = 4096
HALF = D // 2
TOK = 56
SEED = 2 * TOK
CLASS_TOK = 1792
ROWS = 224
HROWS = ROWS // 2
TILE = 512
TILES = D // TILE
MESH = pl.DeviceIdType.MESH
ANY = pl.BlockSpec(memory_space=pl.ANY)


def where_am_i():
    rep, at = lax.axis_index("rep"), lax.axis_index("fsdp")
    return rep // 2, rep % 2, at // 16, (at // 4) % 4, at % 4


def device(zh, c, y, x, z):
    return (zh * 2 + c, (y * 4 + x) * 4 + z)


def barrier(peers):
    sem = pltpu.get_barrier_semaphore()
    for peer in peers:
        pl.semaphore_signal(sem, inc=1, device_id=peer, device_id_type=MESH)
    pl.semaphore_wait(sem, len(peers))


def remote(src, dst, send_sem, recv_sem, peer):
    return pltpu.make_async_remote_copy(src, dst, send_sem, recv_sem, device_id=peer, device_id_type=MESH)


def slope(p):
    s = jax.nn.sigmoid(p)
    return s * (1.0 + p * (1.0 - s))


def work_kernel(f_ref, w_ref, d_ref, m_ref, e_ref, np_ref, nm_ref,
                xs, seed, wv, dv, acc, pre, ht, got, terms, mom, rows_in, rows_out, up, down,
                seed_send, seed_recv, zsend, zrecv, ysend, yrecv, csend, crecv, wsend, wrecv, dsend, drecv, local,
                psend, precv, plocal, fsend, frecv, bsend, brecv, out):
    zh, c, y, x, z = where_am_i()

    def at_y(k):
        return device(zh, c, (y + k) % 4, x, z)

    sibling = device(zh, 1 - c, y, x, z)
    peers = [sibling, at_y(1), at_y(3)]
    peers += [device(zh, c, y, x, (z + k) % 4) for k in range(1, 4)]
    peers += [device(zh, k, y, (x + q) % 4, z) for q in range(1, 4) for k in range(2)]
    keep_w = pltpu.make_async_copy(w_ref, wv.at[pl.ds(0, ROWS)], local.at[1])

    @pl.when(c == 0)
    def _():
        keep_w.start()

    other_half = device(1 - zh, c, y, x, z)
    barrier(peers + [other_half])
    loads = [pltpu.make_async_copy(m_ref, mom, local.at[4]), pltpu.make_async_copy(w_ref, rows_in, local.at[5])]
    for load in loads:
        load.start()

    mirror = 3 - x
    slot = x // 2
    whole = f_ref.at[:, pl.ds(0, HALF)]

    def half(k):
        return f_ref.at[:, pl.ds(pl.multiple_of(k * HALF, HALF), HALF)]

    @pl.when(c == slot)
    def _():
        keep = pltpu.make_async_copy(half(c), seed.at[slot], local.at[0])
        give = remote(half(1 - c), seed.at[slot], seed_send.at[0], seed_recv.at[slot], sibling)
        keep.start()
        give.start()
        keep.wait()
        give.wait_send()
        remote(whole, seed.at[1 - slot], seed_send.at[0], seed_recv.at[1 - slot], sibling).wait_recv()

    @pl.when(c != slot)
    def _():
        sends = [remote(half(k), seed.at[slot], seed_send.at[k], seed_recv.at[slot], device(zh, k, y, mirror, z)) for k in range(2)]
        for s in sends:
            s.start()
        for s in sends:
            s.wait_send()
        for k in range(2):
            remote(whole, seed.at[k], seed_send.at[0], seed_recv.at[k], sibling).wait_recv()

    def place(yy, zz, core, lo=0, n=SEED):
        return xs.at[core, pl.ds(pl.multiple_of((yy * 4 + zz) * SEED + lo, 16), n)]

    joined = jnp.concatenate([seed[0].astype(jnp.float32), seed[1].astype(jnp.float32)], axis=0)
    xs[c, pl.ds(pl.multiple_of((y * 4 + z) * SEED, 16), SEED), :] = joined.astype(jnp.bfloat16)
    own = place(y, z, c)

    zs = [remote(own, own, zsend.at[k], zrecv.at[k], device(zh, c, y, x, (z + k) % 4)) for k in range(1, 4)]
    for s in zs:
        s.start()

    def pass_on(k, zz):
        src = place(y, zz, c)
        remote(src, src, ysend.at[k, 0], yrecv.at[k, 0], at_y(1)).start()
        remote(src, src, ysend.at[k, 1], yrecv.at[k, 1], at_y(3)).start()
        remote(src, src, csend.at[k, 0], crecv.at[k, 0], sibling).start()

    pass_on(0, z)

    ws = []
    for d in range(1, 4):
        src = w_ref.at[pl.ds(pl.multiple_of(c * HROWS, 16), HROWS)]
        dst = wv.at[pl.ds(pl.multiple_of((d % 2) * ROWS + c * HROWS, 16), HROWS)]
        ws.append(remote(src, dst, wsend.at[d], wrecv.at[d % 2, c], device(zh, d // 2, y, (x + 4 - d) % 4, z)))
    for s in ws:
        s.start()

    def dy_of(k):
        to = 2 * c + k
        d = (x - to + 4) % 4
        outer = (to == 0) | (to == 3)
        sets = [jnp.where(outer, 0, 1), jnp.where(outer, 3, 2)]
        return to, d, sets, (d == 0) & (c == 0)

    for k in range(2):
        to, d, sets, mine = dy_of(k)
        for i in range(2):
            @pl.when(mine)
            def _():
                pltpu.make_async_copy(d_ref.at[:, sets[i]], dv.at[0, i], local.at[2 + i]).start()

            @pl.when(jnp.logical_not(mine))
            def _():
                remote(d_ref.at[:, sets[i]], dv.at[d % 2, i], dsend.at[k, i], drecv.at[d % 2, i], device(zh, d // 2, y, to, z)).start()

    def wait_w_and_dy():
        rows = pl.ds(0, HROWS)
        for j in range(2):
            remote(w_ref.at[rows], wv.at[rows], wsend.at[0], wrecv.at[1, j], sibling).wait_recv()

        @pl.when(c == 0)
        def _():
            keep_w.wait()

        @pl.when(c == 1)
        def _():
            for j in range(2):
                remote(w_ref.at[rows], wv.at[rows], wsend.at[0], wrecv.at[0, j], sibling).wait_recv()

        here = (c == 0) & (x // 2 == 0)
        for i in range(2):
            @pl.when(here)
            def _():
                pltpu.make_async_copy(d_ref.at[:, 0], dv.at[0, i], local.at[2 + i]).wait()

            @pl.when(jnp.logical_not(here))
            def _():
                remote(d_ref.at[:, 0], dv.at[0, i], dsend.at[0, i], drecv.at[0, i], sibling).wait_recv()

            remote(d_ref.at[:, 0], dv.at[1, i], dsend.at[0, i], drecv.at[1, i], sibling).wait_recv()

    cut = 64

    def forward(k):
        zz = (z + 4 - k) % 4
        up, down = (y + 3) % 4, (y + 1) % 4
        remote(own, place(up, zz, c), ysend.at[k, 0], yrecv.at[k, 0], at_y(1)).wait_recv()
        src = place(up, zz, c, 0, cut)
        remote(src, src, ysend.at[k, 2], yrecv.at[k, 2], at_y(1)).start()
        src = place(up, zz, c)
        remote(src, src, csend.at[k, 1], crecv.at[k, 1], sibling).start()
        remote(own, place(down, zz, c), ysend.at[k, 1], yrecv.at[k, 1], at_y(3)).wait_recv()
        src = place(down, zz, c, cut, SEED - cut)
        remote(src, src, ysend.at[k, 3], yrecv.at[k, 3], at_y(3)).start()
        src = place(down, zz, c)
        remote(src, src, csend.at[k, 2], crecv.at[k, 2], sibling).start()

    def from_sibling(j):
        for k in range(4):
            remote(own, own, csend.at[k, j], crecv.at[k, j], sibling).wait_recv()

    def partial_parts(t):
        for k in range(2):
            d = 2 * c + k
            src = wv.at[pl.ds(k * ROWS, ROWS), pl.ds(pl.multiple_of(t * TILE, TILE), TILE)]
            to = device(zh, t % 2, y, (x + d) % 4, z)
            yield k, d, src, to, (d == 0) & (c == t % 2)

    def send_partials(t):
        for k, d, src, to, mine in partial_parts(t):
            @pl.when(mine)
            def _():
                pltpu.make_async_copy(src, got.at[t // 2, x], plocal.at[t // 2]).start()

            @pl.when(jnp.logical_not(mine))
            def _():
                remote(src, got.at[t // 2, x], psend.at[k, t], precv.at[t // 2, (4 - d) % 4], to).start()

    def compute(yy, first, last):
        rows = pl.ds(pl.multiple_of(yy * 448, 448), 448)
        pre[...] = jnp.zeros_like(pre)
        for h in range(2):
            @pl.loop(0, 4)
            def _(t):
                cols = pl.ds(pl.multiple_of(t * 512, 512), 512)
                wide = pl.ds(pl.multiple_of(h * HALF + t * 512, 512), 512)
                xt = xs[h, rows, cols]
                for k in range(2):
                    wt = wv[pl.ds(k * ROWS, ROWS), wide]
                    pre[k] += lax.dot_general(xt, wt, (((1,), (1,)), ((), ())), preferred_element_type=jnp.float32)
        for k in range(2):
            dy = [dv[k, i, yy].astype(jnp.float32) for i in range(2)]
            dy = jnp.concatenate([dy[i][zz * TOK:(zz + 1) * TOK] for zz in range(4) for i in range(2)], axis=0)
            hid = dy * slope(pre[k])
            ht[pl.ds(k * ROWS, ROWS), :] = hid.T.astype(jnp.bfloat16)
        for h in range(2):
            @pl.loop(0, 4)
            def _(t):
                cols = pl.ds(pl.multiple_of(t * 512, 512), 512)
                wide = pl.ds(pl.multiple_of(h * HALF + t * 512, 512), 512)
                g = jnp.dot(ht[...], xs[h, rows, cols], preferred_element_type=jnp.float32)
                if not first:
                    g = g + acc[:, wide]
                if not last:
                    acc[:, wide] = g
                else:
                    wv[:, wide] = g.astype(jnp.bfloat16)
                    send_partials(h * 4 + t)

    power = e_ref[...].astype(jnp.float32)
    bigger, smaller = jnp.exp2(power), jnp.exp2(-power)
    for b in range(D // 128):
        cols = pl.ds(b * 128, 128)
        up[:, cols] = jnp.broadcast_to(bigger[:, b:b + 1], (ROWS, 128)).astype(jnp.bfloat16)
        down[:, cols] = jnp.broadcast_to(smaller[:, b:b + 1], (ROWS, 128)).astype(jnp.bfloat16)

    for k in (1, 3, 2):
        remote(own, own, zsend.at[k], zrecv.at[k], sibling).wait_recv()
        pass_on(k, (z + 4 - k) % 4)
    forward(0)
    forward(1)
    wait_w_and_dy()
    from_sibling(0)
    compute(y, True, False)
    forward(3)
    forward(2)
    from_sibling(1)
    compute((y + 3) % 4, False, False)
    for k in (0, 1, 3, 2):
        zz = (z + 4 - k) % 4
        far = (y + 2) % 4
        src = place(far, zz, c, 0, cut)
        remote(src, src, ysend.at[k, 2], yrecv.at[k, 2], at_y(1)).wait_recv()
        src = place(far, zz, c, cut, SEED - cut)
        remote(src, src, ysend.at[k, 3], yrecv.at[k, 3], at_y(3)).wait_recv()
        src = place(far, zz, c)
        remote(src, src, csend.at[k, 3], crecv.at[k, 3], sibling).start()
    from_sibling(2)
    compute((y + 1) % 4, False, False)
    from_sibling(3)
    for k in range(4):
        for j in range(4):
            remote(own, own, csend.at[k, j], crecv.at[k, j], sibling).wait_send()
        for j, n in ((0, SEED), (1, SEED), (2, cut), (3, SEED - cut)):
            src = place(y, z, c, 0, n)
            remote(src, src, ysend.at[k, j], yrecv.at[k, j], sibling).wait_send()
    for s in zs + ws:
        s.wait_send()
    for k in range(2):
        to, d, sets, mine = dy_of(k)
        for i in range(2):
            @pl.when(jnp.logical_not(mine))
            def _():
                remote(d_ref.at[:, 0], dv.at[0, i], dsend.at[k, i], drecv.at[0, i], sibling).wait_send()
    compute((y + 2) % 4, False, True)
    piece = wv.at[pl.ds(0, ROWS), pl.ds(0, TILE)]
    owned = got.at[0, 0]
    crossing = []
    for i in range(TILES // 2):
        t = 2 * i + c
        cols = pl.ds(pl.multiple_of(t * TILE, TILE), TILE)
        for q in range(1, 4):
            remote(piece, owned, psend.at[0, 0], precv.at[i, q], sibling).wait_recv()

        @pl.when(c == 0)
        def _():
            pltpu.make_async_copy(piece, owned, plocal.at[i]).wait()

        @pl.when(c == 1)
        def _():
            remote(piece, owned, psend.at[0, 0], precv.at[i, 0], sibling).wait_recv()

        shrink = down[:, cols].astype(jnp.float32)

        def coded(g):
            total = got[i, 2 * g].astype(jnp.float32) + got[i, 2 * g + 1].astype(jnp.float32)
            return jnp.clip(inner_rate * (total * shrink), -code_limit, code_limit).astype(jnp.bfloat16).astype(jnp.float32)

        terms[t, zh] = (coded(0) + coded(1)).astype(jnp.bfloat16)
        here = terms.at[t, zh]
        over = remote(here, here, fsend.at[i], frecv.at[i], other_half)
        beside = remote(here, here, bsend.at[i, 0], brecv.at[i, 0], sibling)
        over.start()
        beside.start()
        crossing += [over, beside]
    for load in loads:
        load.wait()

    def finish(t, slot):
        cols = pl.ds(pl.multiple_of(t * TILE, TILE), TILE)
        total = terms[t, 0].astype(jnp.float32) + terms[t, 1].astype(jnp.float32)
        decoded = total * up[:, cols].astype(jnp.float32) / 4.0
        new_moment = momentum_coef * mom[:, cols] + decoded
        mom[:, cols] = new_moment
        rows_out[:, cols] = (rows_in[:, cols].astype(jnp.float32) - outer_rate * (decoded + momentum_coef * new_moment)).astype(jnp.bfloat16)
        writes = [pltpu.make_async_copy(mom.at[:, cols], nm_ref.at[:, cols], out.at[slot, 0]),
                  pltpu.make_async_copy(rows_out.at[:, cols], np_ref.at[:, cols], out.at[slot, 1])]
        for write in writes:
            write.start()
        return writes

    writes = []
    for i in range(TILES // 2):
        t, u = 2 * i + c, 2 * i + 1 - c
        remote(owned, owned, fsend.at[i], frecv.at[i], other_half).wait_recv()
        there = terms.at[t, 1 - zh]
        after = remote(there, there, bsend.at[i, 1], brecv.at[i, 1], sibling)
        after.start()
        crossing.append(after)
        writes += finish(t, 2 * i)
        for j in range(2):
            remote(owned, owned, bsend.at[i, j], brecv.at[i, j], sibling).wait_recv()
        writes += finish(u, 2 * i + 1)
    for s in crossing:
        s.wait_send()
    for t in range(TILES):
        for k, d, src, to, mine in partial_parts(t):
            @pl.when(jnp.logical_not(mine))
            def _():
                remote(src, owned, psend.at[k, t], precv.at[0, 0], sibling).wait_send()
    for write in writes:
        write.wait()


DMA = pltpu.SemaphoreType.DMA


def per_device(features, cotangent, up_rows, moment, exponents):
    bf16 = jnp.bfloat16
    dy = cotangent.reshape(4, 4, ROWS, ROWS)
    f32 = jnp.float32
    return pl.pallas_call(
        work_kernel,
        out_shape=[jax.ShapeDtypeStruct((ROWS, D), bf16), jax.ShapeDtypeStruct((ROWS, D), f32)],
        in_specs=[ANY] * 4 + [pl.BlockSpec(memory_space=pltpu.VMEM)], out_specs=[ANY] * 2,
        scratch_shapes=[
            pltpu.VMEM((2, CLASS_TOK, HALF), bf16), pltpu.VMEM((2, TOK, HALF), bf16), pltpu.VMEM((2 * ROWS, D), bf16),
            pltpu.VMEM((2, 2, 4, ROWS, ROWS), bf16), pltpu.VMEM((2 * ROWS, D), f32),
            pltpu.VMEM((2, 448, ROWS), f32), pltpu.VMEM((2 * ROWS, 448), bf16),
            pltpu.VMEM((TILES // 2, 4, ROWS, TILE), bf16), pltpu.VMEM((TILES, 2, ROWS, TILE), bf16),
            pltpu.VMEM((ROWS, D), f32), pltpu.VMEM((ROWS, D), bf16), pltpu.VMEM((ROWS, D), bf16),
            pltpu.VMEM((ROWS, D), bf16), pltpu.VMEM((ROWS, D), bf16),
            DMA((2,)), DMA((2,)), DMA((4,)), DMA((4,)), DMA((4, 4)), DMA((4, 4)), DMA((4, 4)), DMA((4, 4)),
            DMA((4,)), DMA((2, 2)), DMA((2, 2)), DMA((2, 2)), DMA((6,)),
            DMA((2, TILES)), DMA((TILES // 2, 4)), DMA((TILES // 2,)), DMA((TILES // 2,)), DMA((TILES // 2,)),
            DMA((TILES // 2, 2)), DMA((TILES // 2, 2)), DMA((TILES, 2))],
        compiler_params=pltpu.CompilerParams(collective_id=0, has_side_effects=True, vmem_limit_bytes=60 * 2**20), name="work",
    )(features, up_rows, dy, moment, exponents)


def solution(mesh):
    return jax.shard_map(
        per_device,
        mesh=mesh,
        in_specs=(P(("rep", "fsdp"), None), P("rep", "fsdp"), P("fsdp", None), P("fsdp", None), P("fsdp", None)),
        out_specs=(P("fsdp", None), P("fsdp", None)),
        check_vma=False,
    )
```

time: 804 us -> 178 us (0.22)
  waiting for transfers between devices: 737 us -> 0 us
  Pallas kernels: 0 us -> 166 us
  matrix products: 35.4 us -> 0 us
  between operations: 14.1 us -> 0.65 us
  other arithmetic: 10.1 us -> 0 us
    all_gather x1 -> x0, waiting for transfers between devices: 645 us -> none  [per_device(): inputs = lax.all_gather(features, 'fsdp', axis=0, tiled=True)]
    pallas_call x0 -> x1, Pallas kernels: none -> 166 us  [per_device(): pl.pallas_call(work_kernel, out_shape=[jax.ShapeDtypeStruct((ROWS, D), bf...]
    psum x1 -> x0, waiting for transfers between devices: 90.9 us -> none  [per_device(): summed = lax.psum(encoded.astype(jnp.bfloat16), 'rep').astype(jnp.float32)]
    dot_general x1 -> x0, matrix products: 35.4 us -> none  [per_device(): jnp.einsum('tf,td->fd', hidden_grad, inputs, preferred_element_type=jnp.f...]
    convert_element_type x2 -> x0, other arithmetic: 9.33 us -> none  [the longest x1 7.97 us: nesterov_step(): new_params = (params.astype(jnp.float32) - outer_rate * (decoded + moment...]
  transfers between devices with their start and end apart: 2 -> 0, of which waited for: 2 -> 0; matrix products, arithmetic and copies ran while one was open for 0% -> 0% of each run, Pallas kernels for 0% -> 0%
where the time goes in v1:
time: 178 us; the launch traced here: 176 us
  Pallas kernels  166 us (93%)
  local copies, waits for them, and re-layouts  10.1 us (6%)
    pallas_call x1, Pallas kernels, per_device(): pl.pallas_call(work_kernel, out_shape=[jax.ShapeDtypeStruct((ROWS, D), bf...  166 us
    unnamed x6, local copies, waits for them, and re-layouts  10.1 us

profile of v1, /device:TPU:1, one launch (start us, length us, event | category | flops | bytes accessed | tf_op | source)
XLA Modules:
  0.0 176.3 jit_solution(14166297967484441303)
XLA Ops:
  0.6 1.5 copy.8.e_ref
  2.1 3.7 %copy.7 = bf16[3584,224]{1,0:T(8,128)(2,1)} copy(bf16[3584,224]{0,1:T(8,128)(2,1)} %param.6) | data formatting | bytes 3211264 | tf_op args[1]
  5.8 165.5 %work.1 = (bf16[224,4096]{1,0:T(8,128)(2,1)}, f32[224,4096]{1,0:T(8,128)}) custom-call(bf16[56,4096]{1,0:T(8,128)(2,1)} %f_ref.1, bf16[224,4096]{1,0:T(8,128)(2,1)} %w_ref.1, bf16[4,4,224,224]{3,2,1,0:T(8,128)(2,1)} %bitcast.1, f32[224,4096]{1,0:T(8,128)} %m_ref.1, s32[224,32]{1,0:T(8,128)} %copy.8.e_ref), custom_call_target="tpu_custom_call" | custom-call | tf_op jit(solution)/shard_map/work/pallas_call | solution.py:366
  171.4 0.0 copy-start
  171.4 3.1 %copy.11 = bf16[224,4096]{1,0:T(8,128)(2,1)} copy(bf16[224,4096]{1,0:T(8,128)(2,1)} %get-tuple-element.4) | data formatting | bytes 3670016
  174.5 0.0 copy-done
  174.5 1.8 %copy.12 = f32[224,4096]{1,0:T(8,128)} copy(f32[224,4096]{1,0:T(8,128)S(1)} %copy-done) | data formatting | bytes 7340032
Async XLA Ops:
  171.4 3.1 %copy-start = (f32[224,4096]{1,0:T(8,128)S(1)}, f32[224,4096]{1,0:T(8,128)}, u32[]{:S(2)}) copy-start(f32[224,4096]{1,0:T(8,128)} %get-tuple-element.5) | copy-start | bytes 11010052

commit v2 on v1

v2 whole, which is shorter than its diff:
```python
import functools

import jax
import jax.numpy as jnp
from jax import lax
from jax.experimental import pallas as pl
from jax.experimental.pallas import tpu as pltpu
from jax.sharding import PartitionSpec as P

inner_rate = 0.02
outer_rate = 0.7
momentum_coef = 0.9
code_limit = 448.0

D = 4096
HALF = D // 2
TOK = 56
SEED = 2 * TOK
LATE = 16
SOON = SEED - LATE
WIDE = 1024
TOKENS = 3584
ROWS = 224
HROWS = ROWS // 2
TILE = 256
TILES = D // TILE
MESH = pl.DeviceIdType.MESH
ANY = pl.BlockSpec(memory_space=pl.ANY)


def where_am_i():
    rep, at = lax.axis_index("rep"), lax.axis_index("fsdp")
    return rep // 2, rep % 2, at // 16, (at // 4) % 4, at % 4


def device(zh, c, y, x, z):
    return (zh * 2 + c, (y * 4 + x) * 4 + z)


def barrier(peers):
    sem = pltpu.get_barrier_semaphore()
    for peer in peers:
        pl.semaphore_signal(sem, inc=1, device_id=peer, device_id_type=MESH)
    pl.semaphore_wait(sem, len(peers))


def remote(src, dst, send_sem, recv_sem, peer):
    return pltpu.make_async_remote_copy(src, dst, send_sem, recv_sem, device_id=peer, device_id_type=MESH)


def slope(p):
    s = jax.nn.sigmoid(p)
    return s * (1.0 + p * (1.0 - s))


def work_kernel(f_ref, w_ref, d_ref, m_ref, e_ref, np_ref, nm_ref,
                xs, seed, wv, dv, acc, pre, ht, got, terms, mom, rows_in, rows_out, up, down, dt, turned, dn,
                seed_send, seed_recv, zsend, zrecv, ysend, yrecv, csend, crecv, lysend, lyrecv, lzsend, lzrecv, lcsend, lcrecv, wsend, wrecv, dsend, drecv, dlocal, local,
                psend, precv, plocal, fsend, frecv, bsend, brecv, out):
    zh, c, y, x, z = where_am_i()

    def at_y(k):
        return device(zh, c, (y + k) % 4, x, z)

    sibling = device(zh, 1 - c, y, x, z)
    peers = [sibling, at_y(1), at_y(3)]
    peers += [device(zh, c, y, x, (z + k) % 4) for k in range(1, 4)]
    peers += [device(zh, k, y, (x + q) % 4, z) for q in range(1, 4) for k in range(2)]
    keep_w = pltpu.make_async_copy(w_ref, wv.at[pl.ds(0, ROWS)], local.at[1])

    load_d = pltpu.make_async_copy(d_ref, dt, local.at[0])
    load_d.start()

    @pl.when(c == 0)
    def _():
        keep_w.start()

    other_half = device(1 - zh, c, y, x, z)
    barrier(peers + [other_half])
    loads = [pltpu.make_async_copy(m_ref, mom, local.at[4]), pltpu.make_async_copy(w_ref, rows_in, local.at[5])]
    for load in loads:
        load.start()

    mirror = 3 - x
    slot = x // 2
    whole = f_ref.at[:, pl.ds(0, HALF)]

    def half(k):
        return f_ref.at[:, pl.ds(pl.multiple_of(k * HALF, HALF), HALF)]

    keep = pltpu.make_async_copy(half(c), seed.at[slot], local.at[6])
    give = remote(half(1 - c), seed.at[slot], seed_send.at[0], seed_recv.at[slot], sibling)
    across = [remote(half(k), seed.at[slot], seed_send.at[k], seed_recv.at[slot], device(zh, k, y, mirror, z)) for k in range(2)]

    @pl.when(c == slot)
    def _():
        keep.start()
        give.start()

    @pl.when(c != slot)
    def _():
        for s in across:
            s.start()

    near = []
    for k in range(2):
        src = w_ref.at[pl.ds(pl.multiple_of(c * HROWS, 16), HROWS)]
        dst = wv.at[pl.ds(pl.multiple_of((1 - k) * ROWS + c * HROWS, 16), HROWS)]
        near.append(remote(src, dst, wsend.at[k], wrecv.at[1 - k, c], device(zh, k, y, (x + 3 + 2 * k) % 4, z)))

    for k in range(2):
        @pl.when(x % 2 != k)
        def _():
            near[k].start()

    load_d.wait()
    for b in range(TOKENS // 256):
        turned[pl.ds(b * 256, 256), :] = dt[:, pl.ds(b * 256, 256)].astype(jnp.float32).T

    @pl.when(c == slot)
    def _():
        keep.wait()
        give.wait_send()
        remote(whole, seed.at[1 - slot], seed_send.at[0], seed_recv.at[1 - slot], sibling).wait_recv()

    @pl.when(c != slot)
    def _():
        for s in across:
            s.wait_send()
        for k in range(2):
            remote(whole, seed.at[k], seed_send.at[0], seed_recv.at[k], sibling).wait_recv()

    def place(yy, zz, core, lo=0, n=SOON):
        return xs.at[core, zz, yy, pl.ds(lo, n)]

    joined = jnp.concatenate([seed[0].astype(jnp.float32), seed[1].astype(jnp.float32)], axis=0)
    xs[c, z, y] = joined.astype(jnp.bfloat16)
    own = place(y, z, c)

    inner = (z == 1) | (z == 2)
    order = [z, z + 1 - 2 * (z % 2), jnp.where(z < 2, 2, 1), jnp.where(z < 2, 3, 0)]

    def at_z(zz):
        return device(zh, c, y, x, zz)

    @pl.when(z < 3)
    def _():
        remote(own, own, zsend.at[0], zrecv.at[z], at_z(z + 1)).start()

    @pl.when(z > 0)
    def _():
        remote(own, own, zsend.at[1], zrecv.at[z], at_z(z - 1)).start()

    def pass_on(n):
        zz = order[n]
        src = place(y, zz, c)
        remote(src, src, ysend.at[n, 0], yrecv.at[zz, 0], at_y(1)).start()
        remote(src, src, ysend.at[n, 1], yrecv.at[zz, 1], at_y(3)).start()
        remote(src, src, csend.at[n, 0], crecv.at[zz, 0], sibling).start()

    def from_z(n):
        src = place(y, order[n], c)
        remote(src, src, zsend.at[1 + n], zrecv.at[order[n]], sibling).wait_recv()

        @pl.when(inner)
        def _():
            to = 3 - z if n == 1 else jnp.where(z == 1, 0, 3)
            remote(src, src, zsend.at[1 + n], zrecv.at[order[n]], at_z(to)).start()

        pass_on(n)

    def late(yy, k=None):
        if k is None:
            return xs.at[c, z, yy, pl.ds(SOON, LATE)]
        return xs.at[c, z, yy, pl.ds(SOON, LATE), pl.ds(k * (HALF // 2), HALF // 2)]

    def late_y(j):
        src = [late(y), late(y), late((y + 3) % 4, 0), late((y + 1) % 4, 1)][j]
        return remote(src, src, lysend.at[j], lyrecv.at[j], at_y(1 if j % 2 == 0 else 3))

    def late_block(zz):
        return xs.at[c, zz, :, pl.ds(SOON, LATE)]

    def late_z(k, zz, to):
        return remote(late_block(zz), late_block(zz), lzsend.at[k], lzrecv.at[zz], to)

    def late_share(n):
        src = late_block(order[n])
        remote(src, src, lcsend.at[n], lcrecv.at[order[n]], sibling).start()

    def late_from_z(n):
        late_z(1 + n, order[n], sibling).wait_recv()

        @pl.when(inner)
        def _():
            late_z(1 + n, order[n], at_z(3 - z if n == 1 else jnp.where(z == 1, 0, 3))).start()

        late_share(n)

    late_y(0).start()
    late_y(1).start()
    pass_on(0)

    def w_forward():
        row = (1 - c) * HROWS
        src = wv.at[pl.ds(pl.multiple_of((1 - c) * ROWS + row, 16), HROWS)]
        dst = wv.at[pl.ds(pl.multiple_of(ROWS + row, 16), HROWS)]
        return remote(src, dst, wsend.at[2], wrecv.at[1, 1 - c], device(zh, 1, y, (x + 3 + 2 * c) % 4, z))

    def forward_w():
        remote(w_ref.at[pl.ds(0, HROWS)], wv.at[pl.ds(0, HROWS)], wsend.at[2], wrecv.at[1 - c, 1 - c], sibling).wait_recv()
        w_forward().start()

    def wait_w():
        def arrived(k, j):
            remote(w_ref.at[pl.ds(0, HROWS)], wv.at[pl.ds(0, HROWS)], wsend.at[2], wrecv.at[k, j], sibling).wait_recv()

        arrived(1 - c, c)

        @pl.when(c == 0)
        def _():
            keep_w.wait()

        @pl.when(c == 1)
        def _():
            arrived(1, 0)
            arrived(1, 1)

    def make_dy(zz):
        for h, pair in enumerate(((0, 3), (1, 2))):
            for yy in range(4):
                both = [turned[pl.ds(pl.multiple_of(((yy * 4 + at) * 4 + zz) * TOK, 8), TOK), :] for at in pair]
                dn[h, zz, yy] = jnp.concatenate(both, axis=0).astype(jnp.bfloat16)

    def dy_parts(zz):
        for k in range(2):
            to = 2 * c + k
            d = (x - to + 4) % 4
            h = jnp.where((to == 0) | (to == 3), 0, 1)
            yield dn.at[h, zz], (d + d // 2) % 2, device(zh, d // 2, y, to, z), k, (d == 0) & (c == 0)

    def send_dy(zz):
        for src, slot_to, to, k, mine in dy_parts(zz):
            @pl.when(mine)
            def _():
                pltpu.make_async_copy(src, dv.at[0, zz], dlocal.at[zz]).start()

            @pl.when(jnp.logical_not(mine))
            def _():
                remote(src, dv.at[slot_to, zz], dsend.at[k, zz], drecv.at[slot_to, zz], to).start()

    def wait_dy(zz):
        here = (c == 0) & (x // 2 == 0)

        @pl.when(here)
        def _():
            pltpu.make_async_copy(dn.at[0, zz], dv.at[0, zz], dlocal.at[zz]).wait()

        @pl.when(jnp.logical_not(here))
        def _():
            remote(dn.at[0, zz], dv.at[0, zz], dsend.at[0, zz], drecv.at[0, zz], sibling).wait_recv()

        remote(dn.at[0, zz], dv.at[1, zz], dsend.at[0, zz], drecv.at[1, zz], sibling).wait_recv()

    for k in range(2):
        @pl.when(x % 2 == k)
        def _():
            near[k].start()

    make_dy(order[0])
    for j in range(2):
        late_y(j).wait_recv()
        late_y(2 + j).start()

    cut = SOON // 2

    def forward(n):
        zz = order[n]
        above, below = (y + 3) % 4, (y + 1) % 4
        remote(own, place(above, zz, c), ysend.at[n, 0], yrecv.at[zz, 0], at_y(1)).wait_recv()
        src = place(above, zz, c, 0, cut)
        remote(src, src, ysend.at[n, 2], yrecv.at[zz, 2], at_y(1)).start()
        src = place(above, zz, c)
        remote(src, src, csend.at[n, 1], crecv.at[zz, 1], sibling).start()
        remote(own, place(below, zz, c), ysend.at[n, 1], yrecv.at[zz, 1], at_y(3)).wait_recv()
        src = place(below, zz, c, cut, SOON - cut)
        remote(src, src, ysend.at[n, 3], yrecv.at[zz, 3], at_y(3)).start()
        src = place(below, zz, c)
        remote(src, src, csend.at[n, 2], crecv.at[zz, 2], sibling).start()

    def from_far(n):
        zz, far = order[n], (y + 2) % 4
        src = place(far, zz, c, 0, cut)
        remote(src, src, ysend.at[n, 2], yrecv.at[zz, 2], at_y(1)).wait_recv()
        src = place(far, zz, c, cut, SOON - cut)
        remote(src, src, ysend.at[n, 3], yrecv.at[zz, 3], at_y(3)).wait_recv()
        src = place(far, zz, c)
        remote(src, src, csend.at[n, 3], crecv.at[zz, 3], sibling).start()

    def from_sibling(n):
        for j in range(4):
            remote(own, own, csend.at[n, j], crecv.at[order[n], j], sibling).wait_recv()

    def partial_parts(t):
        for k in range(2):
            d = k + c * (3 - 2 * k)
            src = wv.at[pl.ds(k * ROWS, ROWS), pl.ds(pl.multiple_of(t * TILE, TILE), TILE)]
            to = device(zh, t % 2, y, (x + d) % 4, z)
            yield k, d, src, to, (d == 0) & (c == t % 2)

    def send_partials(t):
        for k, d, src, to, mine in partial_parts(t):
            @pl.when(mine)
            def _():
                pltpu.make_async_copy(src, got.at[t // 2, x], plocal.at[t // 2]).start()

            @pl.when(jnp.logical_not(mine))
            def _():
                remote(src, got.at[t // 2, x], psend.at[k, t], precv.at[t // 2, (4 - d) % 4], to).start()

    def compute(tokens, x_of, dy_of, first=False, last=False):
        for k in range(2):
            for h in range(2):
                wt = wv[pl.ds(k * ROWS, ROWS), pl.ds(h * HALF, HALF)]
                q = lax.dot_general(x_of(h, slice(None)), wt, (((1,), (1,)), ((), ())), preferred_element_type=jnp.float32)
                if h == 0:
                    pre[k, pl.ds(0, tokens)] = q
                else:
                    pre[k, pl.ds(0, tokens)] += q
        for k in range(2):
            hid = dy_of(k).astype(jnp.float32) * slope(pre[k, pl.ds(0, tokens)])
            ht[pl.ds(k * ROWS, ROWS), pl.ds(0, tokens)] = hid.T.astype(jnp.bfloat16)
        for h in range(2):
            @pl.loop(0, HALF // WIDE)
            def _(t):
                cols = pl.ds(pl.multiple_of(t * WIDE, WIDE), WIDE)
                wide = pl.ds(pl.multiple_of(h * HALF + t * WIDE, WIDE), WIDE)
                g = jnp.dot(ht[:, pl.ds(0, tokens)], x_of(h, cols), preferred_element_type=jnp.float32)
                if not first:
                    g = g + acc[:, wide]
                if not last:
                    acc[:, wide] = g
                else:
                    wv[:, wide] = g.astype(jnp.bfloat16)
                    for j in range(WIDE // TILE):
                        send_partials((h * HALF // WIDE + t) * (WIDE // TILE) + j)

    def compute_soon(zz, first=False, last=False):
        def x_of(h, cols):
            part = xs[h, zz, :, pl.ds(0, SOON), cols]
            return part.reshape(4 * SOON, part.shape[-1])

        def dy_of(k):
            return dv[k, zz, :, pl.ds(0, SOON), :].reshape(4 * SOON, ROWS)

        compute(4 * SOON, x_of, dy_of, first, last)

    def compute_late():
        def x_of(h, cols):
            part = xs[h, :, :, pl.ds(SOON, LATE), cols]
            return part.reshape(16 * LATE, part.shape[-1])

        def dy_of(k):
            return dv[k, :, :, pl.ds(SOON, LATE), :].reshape(16 * LATE, ROWS)

        compute(16 * LATE, x_of, dy_of)

    power = e_ref[...].astype(jnp.float32).T
    bigger, smaller = jnp.exp2(power), jnp.exp2(-power)
    for b in range(D // 128):
        cols = pl.ds(b * 128, 128)
        up[:, cols] = jnp.broadcast_to(bigger[:, b:b + 1], (ROWS, 128)).astype(jnp.bfloat16)
        down[:, cols] = jnp.broadcast_to(smaller[:, b:b + 1], (ROWS, 128)).astype(jnp.bfloat16)

    for j in range(2):
        late_y(2 + j).wait_recv()

    late_share(0)
    for n in range(1, 4):
        make_dy(order[n])
    from_z(1)
    forward(0)
    from_z(2)
    forward_w()
    send_dy(order[0])
    send_dy(order[1])
    forward(1)
    from_z(3)

    @pl.when(z < 3)
    def _():
        late_z(0, z, at_z(z + 1)).start()

    @pl.when(z > 0)
    def _():
        late_z(1, z, at_z(z - 1)).start()

    from_far(0)
    forward(2)
    late_from_z(1)
    wait_w()
    wait_dy(order[0])
    send_dy(order[2])
    send_dy(order[3])
    from_sibling(0)
    compute_soon(order[0], first=True)
    late_from_z(2)
    from_far(1)
    wait_dy(order[1])
    from_sibling(1)
    compute_soon(order[1])
    forward(3)
    late_from_z(3)
    from_far(2)
    wait_dy(order[2])
    from_sibling(2)
    compute_soon(order[2])
    wait_dy(order[3])
    for k in range(4):
        remote(late_block(0), late_block(0), lcsend.at[0], lcrecv.at[k], sibling).wait_recv()
    compute_late()
    from_far(3)
    from_sibling(3)
    w_forward().wait_send()
    compute_soon(order[3], last=True)
    piece = wv.at[pl.ds(0, ROWS), pl.ds(0, TILE)]
    owned = got.at[0, 0]
    crossing = []
    for i in range(TILES // 2):
        t = 2 * i + c
        cols = pl.ds(pl.multiple_of(t * TILE, TILE), TILE)
        for q in range(1, 4):
            remote(piece, owned, psend.at[0, 0], precv.at[i, q], sibling).wait_recv()

        @pl.when(c == 0)
        def _():
            pltpu.make_async_copy(piece, owned, plocal.at[i]).wait()

        @pl.when(c == 1)
        def _():
            remote(piece, owned, psend.at[0, 0], precv.at[i, 0], sibling).wait_recv()

        shrink = down[:, cols].astype(jnp.float32)

        def coded(g):
            total = got[i, 2 * g].astype(jnp.float32) + got[i, 2 * g + 1].astype(jnp.float32)
            return jnp.clip(inner_rate * (total * shrink), -code_limit, code_limit).astype(jnp.bfloat16).astype(jnp.float32)

        terms[t, zh] = (coded(0) + coded(1)).astype(jnp.bfloat16)
        here = terms.at[t, zh]
        over = remote(here, here, fsend.at[i], frecv.at[i], other_half)
        beside = remote(here, here, bsend.at[i, 0], brecv.at[i, 0], sibling)
        over.start()
        beside.start()
        crossing += [over, beside]
    for load in loads:
        load.wait()

    def finish(t, slot):
        cols = pl.ds(pl.multiple_of(t * TILE, TILE), TILE)
        total = terms[t, 0].astype(jnp.float32) + terms[t, 1].astype(jnp.float32)
        decoded = total * up[:, cols].astype(jnp.float32) / 4.0
        new_moment = momentum_coef * mom[:, cols] + decoded
        mom[:, cols] = new_moment
        rows_out[:, cols] = (rows_in[:, cols].astype(jnp.float32) - outer_rate * (decoded + momentum_coef * new_moment)).astype(jnp.bfloat16)
        writes = [pltpu.make_async_copy(mom.at[:, cols], nm_ref.at[:, cols], out.at[slot, 0]),
                  pltpu.make_async_copy(rows_out.at[:, cols], np_ref.at[:, cols], out.at[slot, 1])]
        for write in writes:
            write.start()
        return writes

    writes = []
    for i in range(TILES // 2):
        t, u = 2 * i + c, 2 * i + 1 - c
        remote(owned, owned, fsend.at[i], frecv.at[i], other_half).wait_recv()
        there = terms.at[t, 1 - zh]
        after = remote(there, there, bsend.at[i, 1], brecv.at[i, 1], sibling)
        after.start()
        crossing.append(after)
        writes += finish(t, 2 * i)
        for j in range(2):
            remote(owned, owned, bsend.at[i, j], brecv.at[i, j], sibling).wait_recv()
        writes += finish(u, 2 * i + 1)
    for k in range(4):
        for j in range(4):
            remote(own, own, csend.at[k, j], crecv.at[k, j], sibling).wait_send()
        for j, n in ((0, SOON), (1, SOON), (2, cut), (3, SOON - cut)):
            src = place(y, z, c, 0, n)
            remote(src, src, ysend.at[k, j], yrecv.at[k, j], sibling).wait_send()

    for j in range(4):
        late_y(j).wait_send()
        remote(late_block(0), late_block(0), lcsend.at[j], lcrecv.at[0], sibling).wait_send()

    @pl.when(z < 3)
    def _():
        remote(own, own, zsend.at[0], zrecv.at[z], at_z(z + 1)).wait_send()
        late_z(0, z, at_z(z + 1)).wait_send()

    @pl.when(z > 0)
    def _():
        remote(own, own, zsend.at[1], zrecv.at[z], at_z(z - 1)).wait_send()
        late_z(1, z, at_z(z - 1)).wait_send()

    @pl.when(inner)
    def _():
        for n in range(1, 4):
            remote(own, own, zsend.at[1 + n], zrecv.at[0], sibling).wait_send()
            late_z(1 + n, order[n], sibling).wait_send()

    for s in near:
        s.wait_send()
    for n in range(4):
        for src, slot_to, to, k, mine in dy_parts(order[n]):
            @pl.when(jnp.logical_not(mine))
            def _():
                remote(src, dv.at[0, 0], dsend.at[k, order[n]], drecv.at[0, 0], sibling).wait_send()

    for s in crossing:
        s.wait_send()
    for t in range(TILES):
        for k, d, src, to, mine in partial_parts(t):
            @pl.when(jnp.logical_not(mine))
            def _():
                remote(src, owned, psend.at[k, t], precv.at[0, 0], sibling).wait_send()
    for write in writes:
        write.wait()


DMA = pltpu.SemaphoreType.DMA


def per_device(features, cotangent, up_rows, moment, exponents):
    bf16 = jnp.bfloat16
    f32 = jnp.float32
    return pl.pallas_call(
        work_kernel,
        out_shape=[jax.ShapeDtypeStruct((ROWS, D), bf16), jax.ShapeDtypeStruct((ROWS, D), f32)],
        in_specs=[ANY] * 4 + [pl.BlockSpec(memory_space=pltpu.VMEM)], out_specs=[ANY] * 2,
        scratch_shapes=[
            pltpu.VMEM((2, 4, 4, SEED, HALF), bf16), pltpu.VMEM((2, TOK, HALF), bf16), pltpu.VMEM((2 * ROWS, D), bf16),
            pltpu.VMEM((2, 4, 4, SEED, ROWS), bf16), pltpu.VMEM((2 * ROWS, D), f32),
            pltpu.VMEM((2, 4 * SOON, ROWS), f32), pltpu.VMEM((2 * ROWS, 4 * SOON), bf16),
            pltpu.VMEM((TILES // 2, 4, ROWS, TILE), bf16), pltpu.VMEM((TILES, 2, ROWS, TILE), bf16),
            pltpu.VMEM((ROWS, D), f32), pltpu.VMEM((ROWS, D), bf16), pltpu.VMEM((ROWS, D), bf16),
            pltpu.VMEM((ROWS, D), bf16), pltpu.VMEM((ROWS, D), bf16),
            pltpu.VMEM((ROWS, TOKENS), bf16), pltpu.VMEM((TOKENS, ROWS), f32), pltpu.VMEM((2, 4, 4, SEED, ROWS), bf16),
            DMA((2,)), DMA((2,)), DMA((5,)), DMA((4,)), DMA((4, 4)), DMA((4, 4)), DMA((4, 4)), DMA((4, 4)),
            DMA((4,)), DMA((4,)), DMA((5,)), DMA((4,)), DMA((4,)), DMA((4,)),
            DMA((3,)), DMA((2, 2)), DMA((2, 4)), DMA((2, 4)), DMA((4,)), DMA((7,)),
            DMA((2, TILES)), DMA((TILES // 2, 4)), DMA((TILES // 2,)), DMA((TILES // 2,)), DMA((TILES // 2,)),
            DMA((TILES // 2, 2)), DMA((TILES // 2, 2)), DMA((TILES, 2))],
        compiler_params=pltpu.CompilerParams(collective_id=0, has_side_effects=True, vmem_limit_bytes=60 * 2**20), name="work",
    )(features, up_rows, cotangent.T, moment, exponents.T)


def solution(mesh):
    return jax.shard_map(
        per_device,
        mesh=mesh,
        in_specs=(P(("rep", "fsdp"), None), P("rep", "fsdp"), P("fsdp", None), P("fsdp", None), P("fsdp", None)),
        out_specs=(P("fsdp", None), P("fsdp", None)),
        check_vma=False,
    )
```

time: 178 us -> 153 us (0.86)
  Pallas kernels: 166 us -> 147 us
  local copies, waits for them, and re-layouts: 10.1 us -> 4.91 us
    pallas_call x1, Pallas kernels: 166 us -> 147 us  [per_device(): pl.pallas_call(work_kernel, out_shape=[jax.ShapeDtypeStruct((ROWS, D), bf...]
    unnamed x6 -> x4, local copies, waits for them, and re-layouts: 10.1 us -> 4.91 us
where the time goes in v2:
time: 153 us
  Pallas kernels  147 us (96%)
  local copies, waits for them, and re-layouts  4.91 us (3%)
    pallas_call x1, Pallas kernels, per_device(): pl.pallas_call(work_kernel, out_shape=[jax.ShapeDtypeStruct((ROWS, D), bf...  147 us
    unnamed x4, local copies, waits for them, and re-layouts  4.91 us

profile of v2, /device:TPU:1, one launch (start us, length us, event | category | flops | bytes accessed | tf_op | source)
XLA Modules:
  0.0 153.0 jit_solution(17367647495938210730)
XLA Ops:
  0.6 147.4 %work.1 = (bf16[224,4096]{1,0:T(8,128)(2,1)}, f32[224,4096]{1,0:T(8,128)}) custom-call(bf16[56,4096]{1,0:T(8,128)(2,1)} %f_ref.1, bf16[224,4096]{1,0:T(8,128)(2,1)} %w_ref.1, bf16[224,3584]{1,0:T(8,128)(2,1)} %bitcast.2, f32[224,4096]{1,0:T(8,128)} %m_ref.1, s32[32,224]{1,0:T(8,128)} %bitcast.3), custom_call_target="tpu_custom_call" | custom-call | tf_op jit(solution)/shard_map/work/pallas_call | solution.py:536
  148.1 0.0 copy-start
  148.1 3.1 %copy.9 = bf16[224,4096]{1,0:T(8,128)(2,1)} copy(bf16[224,4096]{1,0:T(8,128)(2,1)} %get-tuple-element.4) | data formatting | bytes 3670016
  151.2 0.0 copy-done
  151.2 1.8 %copy.10 = f32[224,4096]{1,0:T(8,128)} copy(f32[224,4096]{1,0:T(8,128)S(1)} %copy-done) | data formatting | bytes 7340032
Async XLA Ops:
  148.1 3.1 %copy-start = (f32[224,4096]{1,0:T(8,128)S(1)}, f32[224,4096]{1,0:T(8,128)}, u32[]{:S(2)}) copy-start(f32[224,4096]{1,0:T(8,128)} %get-tuple-element.5) | copy-start | bytes 11010052

commit v3 on v2

--- a/solution.py
+++ b/solution.py
@@ -18,6 +18,7 @@
 SEED = 2 * TOK
 LATE = 16
 SOON = SEED - LATE
+EARLY = 48
 WIDE = 1024
 TOKENS = 3584
 ROWS = 224
@@ -58,6 +59,7 @@
                 seed_send, seed_recv, zsend, zrecv, ysend, yrecv, csend, crecv, lysend, lyrecv, lzsend, lzrecv, lcsend, lcrecv, wsend, wrecv, dsend, drecv, dlocal, local,
                 psend, precv, plocal, fsend, frecv, bsend, brecv, out):
     zh, c, y, x, z = where_am_i()
+    role = 1 - c
 
     def at_y(k):
         return device(zh, c, (y + k) % 4, x, z)
@@ -71,7 +73,7 @@
     load_d = pltpu.make_async_copy(d_ref, dt, local.at[0])
     load_d.start()
 
-    @pl.when(c == 0)
+    @pl.when(role == 0)
     def _():
         keep_w.start()
 
@@ -82,22 +84,22 @@
         load.start()
 
     mirror = 3 - x
-    slot = x // 2
+    owner = c == x // 2
     whole = f_ref.at[:, pl.ds(0, HALF)]
 
     def half(k):
         return f_ref.at[:, pl.ds(pl.multiple_of(k * HALF, HALF), HALF)]
 
-    keep = pltpu.make_async_copy(half(c), seed.at[slot], local.at[6])
-    give = remote(half(1 - c), seed.at[slot], seed_send.at[0], seed_recv.at[slot], sibling)
-    across = [remote(half(k), seed.at[slot], seed_send.at[k], seed_recv.at[slot], device(zh, k, y, mirror, z)) for k in range(2)]
-
-    @pl.when(c == slot)
+    keep = pltpu.make_async_copy(half(c), seed.at[0], local.at[6])
+    give = remote(half(1 - c), seed.at[0], seed_send.at[0], seed_recv.at[0], sibling)
+    across = [remote(half(k), seed.at[1], seed_send.at[k], seed_recv.at[1], device(zh, k, y, mirror, z)) for k in range(2)]
+
+    @pl.when(owner)
     def _():
         keep.start()
         give.start()
 
-    @pl.when(c != slot)
+    @pl.when(jnp.logical_not(owner))
     def _():
         for s in across:
             s.start()
@@ -106,57 +108,62 @@
     for k in range(2):
         src = w_ref.at[pl.ds(pl.multiple_of(c * HROWS, 16), HROWS)]
         dst = wv.at[pl.ds(pl.multiple_of((1 - k) * ROWS + c * HROWS, 16), HROWS)]
-        near.append(remote(src, dst, wsend.at[k], wrecv.at[1 - k, c], device(zh, k, y, (x + 3 + 2 * k) % 4, z)))
+        near.append(remote(src, dst, wsend.at[k], wrecv.at[1 - k, c], device(zh, 1 - k, y, (x + 3 + 2 * k) % 4, z)))
 
     for k in range(2):
         @pl.when(x % 2 != k)
         def _():
             near[k].start()
+
+    def place(yy, zz, core, lo=0, n=SOON):
+        return xs.at[core, zz, yy, pl.ds(lo, n)]
+
+    own = place(y, z, c)
+
+    inner = (z == 1) | (z == 2)
+    order = [z, z + 1 - 2 * (z % 2), jnp.where(z < 2, 2, 1), jnp.where(z < 2, 3, 0)]
+
+    def at_z(zz):
+        return device(zh, c, y, x, zz)
+
+    def send_own(lo, n):
+        src = place(y, z, c, lo, n)
+
+        @pl.when(z < 3)
+        def _():
+            remote(src, src, zsend.at[0], zrecv.at[z], at_z(z + 1)).start()
+
+        @pl.when(z > 0)
+        def _():
+            remote(src, src, zsend.at[1], zrecv.at[z], at_z(z - 1)).start()
+
+        pass_on(0, lo, n)
+
+    def pass_on(n, lo=0, rows=SOON):
+        zz = order[n]
+        src = place(y, zz, c, lo, rows)
+        remote(src, src, ysend.at[n, 0], yrecv.at[zz, 0], at_y(1)).start()
+        remote(src, src, ysend.at[n, 1], yrecv.at[zz, 1], at_y(3)).start()
+        remote(src, src, csend.at[n, 0], crecv.at[zz, 0], sibling).start()
+
+    @pl.when(owner)
+    def _():
+        keep.wait()
+
+    @pl.when(jnp.logical_not(owner))
+    def _():
+        remote(whole, seed.at[0], seed_send.at[0], seed_recv.at[0], sibling).wait_recv()
+
+    xs[c, z, y, pl.ds(0, EARLY)] = seed[0, pl.ds(0, EARLY)]
+    send_own(0, EARLY)
 
     load_d.wait()
     for b in range(TOKENS // 256):
         turned[pl.ds(b * 256, 256), :] = dt[:, pl.ds(b * 256, 256)].astype(jnp.float32).T
-
-    @pl.when(c == slot)
-    def _():
-        keep.wait()
-        give.wait_send()
-        remote(whole, seed.at[1 - slot], seed_send.at[0], seed_recv.at[1 - slot], sibling).wait_recv()
-
-    @pl.when(c != slot)
-    def _():
-        for s in across:
-            s.wait_send()
-        for k in range(2):
-            remote(whole, seed.at[k], seed_send.at[0], seed_recv.at[k], sibling).wait_recv()
-
-    def place(yy, zz, core, lo=0, n=SOON):
-        return xs.at[core, zz, yy, pl.ds(lo, n)]
-
+    remote(whole, seed.at[1], seed_send.at[0], seed_recv.at[1], sibling).wait_recv()
     joined = jnp.concatenate([seed[0].astype(jnp.float32), seed[1].astype(jnp.float32)], axis=0)
-    xs[c, z, y] = joined.astype(jnp.bfloat16)
-    own = place(y, z, c)
-
-    inner = (z == 1) | (z == 2)
-    order = [z, z + 1 - 2 * (z % 2), jnp.where(z < 2, 2, 1), jnp.where(z < 2, 3, 0)]
-
-    def at_z(zz):
-        return device(zh, c, y, x, zz)
-
-    @pl.when(z < 3)
-    def _():
-        remote(own, own, zsend.at[0], zrecv.at[z], at_z(z + 1)).start()
-
-    @pl.when(z > 0)
-    def _():
-        remote(own, own, zsend.at[1], zrecv.at[z], at_z(z - 1)).start()
-
-    def pass_on(n):
-        zz = order[n]
-        src = place(y, zz, c)
-        remote(src, src, ysend.at[n, 0], yrecv.at[zz, 0], at_y(1)).start()
-        remote(src, src, ysend.at[n, 1], yrecv.at[zz, 1], at_y(3)).start()
-        remote(src, src, csend.at[n, 0], crecv.at[zz, 0], sibling).start()
+    xs[c, z, y, pl.ds(EARLY, SEED - EARLY)] = joined[EARLY:].astype(jnp.bfloat16)
+    send_own(EARLY, SOON - EARLY)
 
     def from_z(n):
         src = place(y, order[n], c)
@@ -199,29 +206,28 @@
 
     late_y(0).start()
     late_y(1).start()
-    pass_on(0)
 
     def w_forward():
-        row = (1 - c) * HROWS
-        src = wv.at[pl.ds(pl.multiple_of((1 - c) * ROWS + row, 16), HROWS)]
+        row = (1 - role) * HROWS
+        src = wv.at[pl.ds(pl.multiple_of((1 - role) * ROWS + row, 16), HROWS)]
         dst = wv.at[pl.ds(pl.multiple_of(ROWS + row, 16), HROWS)]
-        return remote(src, dst, wsend.at[2], wrecv.at[1, 1 - c], device(zh, 1, y, (x + 3 + 2 * c) % 4, z))
+        return remote(src, dst, wsend.at[2], wrecv.at[1, 1 - role], device(zh, 0, y, (x + 3 + 2 * role) % 4, z))
 
     def forward_w():
-        remote(w_ref.at[pl.ds(0, HROWS)], wv.at[pl.ds(0, HROWS)], wsend.at[2], wrecv.at[1 - c, 1 - c], sibling).wait_recv()
+        remote(w_ref.at[pl.ds(0, HROWS)], wv.at[pl.ds(0, HROWS)], wsend.at[2], wrecv.at[1 - role, 1 - role], sibling).wait_recv()
         w_forward().start()
 
     def wait_w():
         def arrived(k, j):
             remote(w_ref.at[pl.ds(0, HROWS)], wv.at[pl.ds(0, HROWS)], wsend.at[2], wrecv.at[k, j], sibling).wait_recv()
 
-        arrived(1 - c, c)
-
-        @pl.when(c == 0)
+        arrived(1 - role, role)
+
+        @pl.when(role == 0)
         def _():
             keep_w.wait()
 
-        @pl.when(c == 1)
+        @pl.when(role == 1)
         def _():
             arrived(1, 0)
             arrived(1, 1)
@@ -229,7 +235,8 @@
     def make_dy(zz):
         for h, pair in enumerate(((0, 3), (1, 2))):
             for yy in range(4):
-                both = [turned[pl.ds(pl.multiple_of(((yy * 4 + at) * 4 + zz) * TOK, 8), TOK), :] for at in pair]
+                pair_of = [jnp.where(c == 0, pair[0], pair[1]), jnp.where(c == 0, pair[1], pair[0])]
+                both = [turned[pl.ds(pl.multiple_of(((yy * 4 + at) * 4 + zz) * TOK, 8), TOK), :] for at in pair_of]
                 dn[h, zz, yy] = jnp.concatenate(both, axis=0).astype(jnp.bfloat16)
 
     def dy_parts(zz):
@@ -237,7 +244,7 @@
             to = 2 * c + k
             d = (x - to + 4) % 4
             h = jnp.where((to == 0) | (to == 3), 0, 1)
-            yield dn.at[h, zz], (d + d // 2) % 2, device(zh, d // 2, y, to, z), k, (d == 0) & (c == 0)
+            yield dn.at[h, zz], (d + d // 2) % 2, device(zh, 1 - d // 2, y, to, z), k, (d == 0) & (c == 1)
 
     def send_dy(zz):
         for src, slot_to, to, k, mine in dy_parts(zz):
@@ -250,7 +257,7 @@
                 remote(src, dv.at[slot_to, zz], dsend.at[k, zz], drecv.at[slot_to, zz], to).start()
 
     def wait_dy(zz):
-        here = (c == 0) & (x // 2 == 0)
+        here = (c == 1) & (x // 2 == 1)
 
         @pl.when(here)
         def _():
@@ -303,7 +310,7 @@
 
     def partial_parts(t):
         for k in range(2):
-            d = k + c * (3 - 2 * k)
+            d = k + role * (3 - 2 * k)
             src = wv.at[pl.ds(k * ROWS, ROWS), pl.ds(pl.multiple_of(t * TILE, TILE), TILE)]
             to = device(zh, t % 2, y, (x + d) % 4, z)
             yield k, d, src, to, (d == 0) & (c == t % 2)
@@ -318,7 +325,21 @@
             def _():
                 remote(src, got.at[t // 2, x], psend.at[k, t], precv.at[t // 2, (4 - d) % 4], to).start()
 
-    def compute(tokens, x_of, dy_of, first=False, last=False):
+    def compute(soon=(), late=False, first=False, last=False):
+        tokens = 4 * SOON * len(soon) + 16 * LATE * late
+
+        def x_of(h, cols):
+            parts = [xs[h, order[n], :, pl.ds(0, SOON), cols] for n in soon]
+            if late:
+                parts.append(xs[h, :, :, pl.ds(SOON, LATE), cols])
+            return jnp.concatenate([p.reshape(-1, p.shape[-1]) for p in parts], axis=0)
+
+        def dy_of(k):
+            parts = [dv[k, order[n], :, pl.ds(0, SOON), :] for n in soon]
+            if late:
+                parts.append(dv[k, :, :, pl.ds(SOON, LATE), :])
+            return jnp.concatenate([p.reshape(-1, ROWS) for p in parts], axis=0)
+
         for k in range(2):
             for h in range(2):
                 wt = wv[pl.ds(k * ROWS, ROWS), pl.ds(h * HALF, HALF)]
@@ -345,26 +366,6 @@
                     for j in range(WIDE // TILE):
                         send_partials((h * HALF // WIDE + t) * (WIDE // TILE) + j)
 
-    def compute_soon(zz, first=False, last=False):
-        def x_of(h, cols):
-            part = xs[h, zz, :, pl.ds(0, SOON), cols]
-            return part.reshape(4 * SOON, part.shape[-1])
-
-        def dy_of(k):
-            return dv[k, zz, :, pl.ds(0, SOON), :].reshape(4 * SOON, ROWS)
-
-        compute(4 * SOON, x_of, dy_of, first, last)
-
-    def compute_late():
-        def x_of(h, cols):
-            part = xs[h, :, :, pl.ds(SOON, LATE), cols]
-            return part.reshape(16 * LATE, part.shape[-1])
-
-        def dy_of(k):
-            return dv[k, :, :, pl.ds(SOON, LATE), :].reshape(16 * LATE, ROWS)
-
-        compute(16 * LATE, x_of, dy_of)
-
     power = e_ref[...].astype(jnp.float32).T
     bigger, smaller = jnp.exp2(power), jnp.exp2(-power)
     for b in range(D // 128):
@@ -386,7 +387,6 @@
     send_dy(order[1])
     forward(1)
     from_z(3)
-
     @pl.when(z < 3)
     def _():
         late_z(0, z, at_z(z + 1)).start()
@@ -403,26 +403,24 @@
     send_dy(order[2])
     send_dy(order[3])
     from_sibling(0)
-    compute_soon(order[0], first=True)
     late_from_z(2)
     from_far(1)
     wait_dy(order[1])
     from_sibling(1)
-    compute_soon(order[1])
+    compute((0, 1), first=True)
     forward(3)
     late_from_z(3)
     from_far(2)
     wait_dy(order[2])
     from_sibling(2)
-    compute_soon(order[2])
     wait_dy(order[3])
     for k in range(4):
         remote(late_block(0), late_block(0), lcsend.at[0], lcrecv.at[k], sibling).wait_recv()
-    compute_late()
+    compute((2,), late=True)
     from_far(3)
     from_sibling(3)
     w_forward().wait_send()
-    compute_soon(order[3], last=True)
+    compute((3,), last=True)
     piece = wv.at[pl.ds(0, ROWS), pl.ds(0, TILE)]
     owned = got.at[0, 0]
     crossing = []
@@ -432,11 +430,11 @@
         for q in range(1, 4):
             remote(piece, owned, psend.at[0, 0], precv.at[i, q], sibling).wait_recv()
 
+        @pl.when(c == 1)
+        def _():
+            pltpu.make_async_copy(piece, owned, plocal.at[i]).wait()
+
         @pl.when(c == 0)
-        def _():
-            pltpu.make_async_copy(piece, owned, plocal.at[i]).wait()
-
-        @pl.when(c == 1)
         def _():
             remote(piece, owned, psend.at[0, 0], precv.at[i, 0], sibling).wait_recv()
 
@@ -481,6 +479,15 @@
         for j in range(2):
             remote(owned, owned, bsend.at[i, j], brecv.at[i, j], sibling).wait_recv()
         writes += finish(u, 2 * i + 1)
+    @pl.when(owner)
+    def _():
+        give.wait_send()
+
+    @pl.when(jnp.logical_not(owner))
+    def _():
+        for s in across:
+            s.wait_send()
+
     for k in range(4):
         for j in range(4):
             remote(own, own, csend.at[k, j], crecv.at[k, j], sibling).wait_send()
@@ -540,7 +547,7 @@
         scratch_shapes=[
             pltpu.VMEM((2, 4, 4, SEED, HALF), bf16), pltpu.VMEM((2, TOK, HALF), bf16), pltpu.VMEM((2 * ROWS, D), bf16),
             pltpu.VMEM((2, 4, 4, SEED, ROWS), bf16), pltpu.VMEM((2 * ROWS, D), f32),
-            pltpu.VMEM((2, 4 * SOON, ROWS), f32), pltpu.VMEM((2 * ROWS, 4 * SOON), bf16),
+            pltpu.VMEM((2, 8 * SOON, ROWS), f32), pltpu.VMEM((2 * ROWS, 8 * SOON), bf16),
             pltpu.VMEM((TILES // 2, 4, ROWS, TILE), bf16), pltpu.VMEM((TILES, 2, ROWS, TILE), bf16),
             pltpu.VMEM((ROWS, D), f32), pltpu.VMEM((ROWS, D), bf16), pltpu.VMEM((ROWS, D), bf16),
             pltpu.VMEM((ROWS, D), bf16), pltpu.VMEM((ROWS, D), bf16),

time: 153 us -> 149 us (0.974)
  Pallas kernels: 147 us -> 143 us
    pallas_call x1, Pallas kernels: 147 us -> 143 us  [per_device(): pl.pallas_call(work_kernel, out_shape=[jax.ShapeDtypeStruct((ROWS, D), bf...]
where the time goes in v3:
time: 149 us; the launch traced here: 148 us
  Pallas kernels  143 us (96%)
  local copies, waits for them, and re-layouts  4.91 us (3%)
    pallas_call x1, Pallas kernels, per_device(): pl.pallas_call(work_kernel, out_shape=[jax.ShapeDtypeStruct((ROWS, D), bf...  143 us
    unnamed x4, local copies, waits for them, and re-layouts  4.91 us

profile of v3, /device:TPU:1, one launch (start us, length us, event | category | flops | bytes accessed | tf_op | source)
XLA Modules:
  0.0 148.1 jit_solution(9246249158664845459)
XLA Ops:
  0.6 142.5 %work.1 = (bf16[224,4096]{1,0:T(8,128)(2,1)}, f32[224,4096]{1,0:T(8,128)}) custom-call(bf16[56,4096]{1,0:T(8,128)(2,1)} %f_ref.1, bf16[224,4096]{1,0:T(8,128)(2,1)} %w_ref.1, bf16[224,3584]{1,0:T(8,128)(2,1)} %bitcast.2, f32[224,4096]{1,0:T(8,128)} %m_ref.1, s32[32,224]{1,0:T(8,128)} %bitcast.3), custom_call_target="tpu_custom_call" | custom-call | tf_op jit(solution)/shard_map/work/pallas_call | solution.py:543
  143.2 0.0 copy-start
  143.2 3.1 %copy.9 = bf16[224,4096]{1,0:T(8,128)(2,1)} copy(bf16[224,4096]{1,0:T(8,128)(2,1)} %get-tuple-element.4) | data formatting | bytes 3670016
  146.3 0.0 copy-done
  146.3 1.8 %copy.10 = f32[224,4096]{1,0:T(8,128)} copy(f32[224,4096]{1,0:T(8,128)S(1)} %copy-done) | data formatting | bytes 7340032
Async XLA Ops:
  143.2 3.1 %copy-start = (f32[224,4096]{1,0:T(8,128)S(1)}, f32[224,4096]{1,0:T(8,128)}, u32[]{:S(2)}) copy-start(f32[224,4096]{1,0:T(8,128)} %get-tuple-element.5) | copy-start | bytes 11010052

commit v4 on v3

--- a/solution.py
+++ b/solution.py
@@ -25,6 +25,7 @@
 HROWS = ROWS // 2
 TILE = 256
 TILES = D // TILE
+LAG = 3
 MESH = pl.DeviceIdType.MESH
 ANY = pl.BlockSpec(memory_space=pl.ANY)
 
@@ -423,34 +424,7 @@
     compute((3,), last=True)
     piece = wv.at[pl.ds(0, ROWS), pl.ds(0, TILE)]
     owned = got.at[0, 0]
-    crossing = []
-    for i in range(TILES // 2):
-        t = 2 * i + c
-        cols = pl.ds(pl.multiple_of(t * TILE, TILE), TILE)
-        for q in range(1, 4):
-            remote(piece, owned, psend.at[0, 0], precv.at[i, q], sibling).wait_recv()
-
-        @pl.when(c == 1)
-        def _():
-            pltpu.make_async_copy(piece, owned, plocal.at[i]).wait()
-
-        @pl.when(c == 0)
-        def _():
-            remote(piece, owned, psend.at[0, 0], precv.at[i, 0], sibling).wait_recv()
-
-        shrink = down[:, cols].astype(jnp.float32)
-
-        def coded(g):
-            total = got[i, 2 * g].astype(jnp.float32) + got[i, 2 * g + 1].astype(jnp.float32)
-            return jnp.clip(inner_rate * (total * shrink), -code_limit, code_limit).astype(jnp.bfloat16).astype(jnp.float32)
-
-        terms[t, zh] = (coded(0) + coded(1)).astype(jnp.bfloat16)
-        here = terms.at[t, zh]
-        over = remote(here, here, fsend.at[i], frecv.at[i], other_half)
-        beside = remote(here, here, bsend.at[i, 0], brecv.at[i, 0], sibling)
-        over.start()
-        beside.start()
-        crossing += [over, beside]
+    crossing, writes = [], []
     for load in loads:
         load.wait()
 
@@ -467,18 +441,49 @@
             write.start()
         return writes
 
-    writes = []
-    for i in range(TILES // 2):
+    def finish_pair(i):
         t, u = 2 * i + c, 2 * i + 1 - c
         remote(owned, owned, fsend.at[i], frecv.at[i], other_half).wait_recv()
         there = terms.at[t, 1 - zh]
         after = remote(there, there, bsend.at[i, 1], brecv.at[i, 1], sibling)
         after.start()
         crossing.append(after)
-        writes += finish(t, 2 * i)
+        writes.extend(finish(t, 2 * i))
         for j in range(2):
             remote(owned, owned, bsend.at[i, j], brecv.at[i, j], sibling).wait_recv()
-        writes += finish(u, 2 * i + 1)
+        writes.extend(finish(u, 2 * i + 1))
+
+    for i in range(TILES // 2):
+        t = 2 * i + c
+        cols = pl.ds(pl.multiple_of(t * TILE, TILE), TILE)
+        for q in range(1, 4):
+            remote(piece, owned, psend.at[0, 0], precv.at[i, q], sibling).wait_recv()
+
+        @pl.when(c == 1)
+        def _():
+            pltpu.make_async_copy(piece, owned, plocal.at[i]).wait()
+
+        @pl.when(c == 0)
+        def _():
+            remote(piece, owned, psend.at[0, 0], precv.at[i, 0], sibling).wait_recv()
+
+        shrink = down[:, cols].astype(jnp.float32)
+
+        def coded(g):
+            total = got[i, 2 * g].astype(jnp.float32) + got[i, 2 * g + 1].astype(jnp.float32)
+            return jnp.clip(inner_rate * (total * shrink), -code_limit, code_limit).astype(jnp.bfloat16).astype(jnp.float32)
+
+        terms[t, zh] = (coded(0) + coded(1)).astype(jnp.bfloat16)
+        here = terms.at[t, zh]
+        over = remote(here, here, fsend.at[i], frecv.at[i], other_half)
+        beside = remote(here, here, bsend.at[i, 0], brecv.at[i, 0], sibling)
+        over.start()
+        beside.start()
+        crossing += [over, beside]
+        if i >= LAG:
+            finish_pair(i - LAG)
+    for i in range(TILES // 2 - LAG, TILES // 2):
+        finish_pair(i)
     @pl.when(owner)
     def _():
         give.wait_send()

time: 149 us -> 144 us (0.966)
  Pallas kernels: 143 us -> 138 us
    pallas_call x1, Pallas kernels: 143 us -> 138 us  [per_device(): pl.pallas_call(work_kernel, out_shape=[jax.ShapeDtypeStruct((ROWS, D), bf...]
where the time goes in v4:
time: 144 us
  Pallas kernels  138 us (96%)
  local copies, waits for them, and re-layouts  4.91 us (3%)
    pallas_call x1, Pallas kernels, per_device(): pl.pallas_call(work_kernel, out_shape=[jax.ShapeDtypeStruct((ROWS, D), bf...  138 us
    unnamed x4, local copies, waits for them, and re-layouts  4.91 us

profile of v4, /device:TPU:1, one launch (start us, length us, event | category | flops | bytes accessed | tf_op | source)
XLA Modules:
  0.0 143.9 jit_solution(1329440035843051676)
XLA Ops:
  0.6 138.4 %work.1 = (bf16[224,4096]{1,0:T(8,128)(2,1)}, f32[224,4096]{1,0:T(8,128)}) custom-call(bf16[56,4096]{1,0:T(8,128)(2,1)} %f_ref.1, bf16[224,4096]{1,0:T(8,128)(2,1)} %w_ref.1, bf16[224,3584]{1,0:T(8,128)(2,1)} %bitcast.2, f32[224,4096]{1,0:T(8,128)} %m_ref.1, s32[32,224]{1,0:T(8,128)} %bitcast.3), custom_call_target="tpu_custom_call" | custom-call | tf_op jit(solution)/shard_map/work/pallas_call | solution.py:548
  139.0 0.0 copy-start
  139.0 3.1 %copy.9 = bf16[224,4096]{1,0:T(8,128)(2,1)} copy(bf16[224,4096]{1,0:T(8,128)(2,1)} %get-tuple-element.4) | data formatting | bytes 3670016
  142.1 0.0 copy-done
  142.1 1.8 %copy.10 = f32[224,4096]{1,0:T(8,128)} copy(f32[224,4096]{1,0:T(8,128)S(1)} %copy-done) | data formatting | bytes 7340032
Async XLA Ops:
  139.0 3.1 %copy-start = (f32[224,4096]{1,0:T(8,128)S(1)}, f32[224,4096]{1,0:T(8,128)}, u32[]{:S(2)}) copy-start(f32[224,4096]{1,0:T(8,128)} %get-tuple-element.5) | copy-start | bytes 11010052

commit v5 on v4

--- a/solution.py
+++ b/solution.py
@@ -25,7 +25,7 @@
 HROWS = ROWS // 2
 TILE = 256
 TILES = D // TILE
-LAG = 3
+LAG = 2
 MESH = pl.DeviceIdType.MESH
 ANY = pl.BlockSpec(memory_space=pl.ANY)
 

time: 144 us -> 144 us (level)
  no operation moved by 1% of the time
where the time goes in v5:
time: 144 us
  Pallas kernels  138 us (96%)
  local copies, waits for them, and re-layouts  4.91 us (3%)
    pallas_call x1, Pallas kernels, per_device(): pl.pallas_call(work_kernel, out_shape=[jax.ShapeDtypeStruct((ROWS, D), bf...  138 us
    unnamed x4, local copies, waits for them, and re-layouts  4.91 us

profile of v5, /device:TPU:1, one launch (start us, length us, event | category | flops | bytes accessed | tf_op | source)
XLA Modules:
  0.0 143.9 jit_solution(1730276910155233452)
XLA Ops:
  0.6 138.4 %work.1 = (bf16[224,4096]{1,0:T(8,128)(2,1)}, f32[224,4096]{1,0:T(8,128)}) custom-call(bf16[56,4096]{1,0:T(8,128)(2,1)} %f_ref.1, bf16[224,4096]{1,0:T(8,128)(2,1)} %w_ref.1, bf16[224,3584]{1,0:T(8,128)(2,1)} %bitcast.2, f32[224,4096]{1,0:T(8,128)} %m_ref.1, s32[32,224]{1,0:T(8,128)} %bitcast.3), custom_call_target="tpu_custom_call" | custom-call | tf_op jit(solution)/shard_map/work/pallas_call | solution.py:548
  139.0 0.0 copy-start
  139.0 3.1 %copy.9 = bf16[224,4096]{1,0:T(8,128)(2,1)} copy(bf16[224,4096]{1,0:T(8,128)(2,1)} %get-tuple-element.4) | data formatting | bytes 3670016
  142.1 0.0 copy-done
  142.1 1.8 %copy.10 = f32[224,4096]{1,0:T(8,128)} copy(f32[224,4096]{1,0:T(8,128)S(1)} %copy-done) | data formatting | bytes 7340032
Async XLA Ops:
  139.0 3.1 %copy-start = (f32[224,4096]{1,0:T(8,128)S(1)}, f32[224,4096]{1,0:T(8,128)}, u32[]{:S(2)}) copy-start(f32[224,4096]{1,0:T(8,128)} %get-tuple-element.5) | copy-start | bytes 11010052
